TPU v7x, 32 devices: a whole 2x2x4 slice. The times are simulated.
32 devices in a mesh: groups: 2 (over y), chan: 4 (over z), sub: 2 (over x), rep: 2 (over core).
Axes of the slice: x: 2, y: 2, z: 4, core: 2. Of those that a mesh axis runs over, the one named last changes fastest.
Arguments:
- traces: bfloat16 [512, 128, 512], P(('groups', 'sub', 'rep'), 'chan'), parts along dimension 0, may hold values from -6 to 6
- channel_slot: int32 [512], P(('groups', 'sub', 'rep')), parts along dimension 0, may hold values from 0 to 63, as said below
Outputs:
- correlations: float32 [3, 8, 64, 64, 128], P(None, ('groups', 'chan'), 'sub', 'rep'), parts along dimension 1
There are 2 independent parts, one for each index of `groups`. A program takes and returns all parts, laid end to end along the dimension named above; each array names one. Nothing has to cross between parts.
Inputs may be any that keep to these rules, and one draw needn't show every extreme that they name: `channel_slot`: each aligned run of 64 entries is a permutation of 0 .. 63.
All inputs are finite; a program needn't handle non-finite values.
Results may differ from a plain program's by a relative error of at most 0.0052.
Values may be sent and summed in bfloat16 or wider, within the bound.
No kernel may reach another device: no remote copies, remote signals or barrier semaphores. Data moves between devices by JAX's collectives and lax.ppermute only.
A program may use at most 64 MiB of HBM per device.

v0:
```python
import functools
import math

import jax
import jax.numpy as jnp
import numpy as np
from jax import lax
from jax.experimental import pallas as pl
from jax.experimental.pallas import tpu as pltpu
from jax.sharding import PartitionSpec as P

LAGS = 128
ROUNDS = 3
LANES = 128
HALF = LANES // 2
VMEM_BYTES = 32 * 1024 * 1024
ORDER_VMEM_BYTES = 48 * 1024 * 1024
NT = (((1,), (1,)), ((), ()))
BLOCKS = 4
FAR = (0, 1)
NEAR = (2, 3)
KEPT_AT, OWN_AT = 0, 2


def kernel_call(kernel, name, flops, bytes_accessed, vmem_bytes=VMEM_BYTES, **more):
    return pl.pallas_call(
        kernel,
        name=name,
        compiler_params=pltpu.CompilerParams(vmem_limit_bytes=vmem_bytes),
        cost_estimate=pl.CostEstimate(flops=flops, bytes_accessed=bytes_accessed, transcendentals=0),
        **more,
    )


def in_vmem():
    return pl.BlockSpec(memory_space=pltpu.VMEM)


def dft_rows_table(samples):
    bins = samples // 2
    turns = (np.arange(bins)[:, None] * np.arange(samples)[None, :]) % samples
    angles = turns.astype(np.float32) * np.float32(2.0 * math.pi / samples)
    table = np.concatenate([np.cos(angles), -np.sin(angles)], axis=0)
    return jnp.asarray(table.astype(np.float32)).astype(jnp.bfloat16)


def lag_rows_table(samples, scale):
    bins = samples // 2
    offsets = np.arange(LAGS) - LAGS // 2
    turns = (offsets[:, None] * np.arange(bins)[None, :]) % samples
    angles = turns.astype(np.float32) * np.float32(2.0 * math.pi / samples)
    table = np.concatenate([np.cos(angles), -np.sin(angles)], axis=1) * np.float32(scale)
    return jnp.asarray(table.astype(np.float32)).astype(jnp.bfloat16)


def selection(rows, columns, ones):
    table = np.zeros((rows, columns), np.float32)
    for row, column in ones:
        table[row, column] = 1.0
    return jnp.asarray(table).astype(jnp.bfloat16)


def own_picks():
    piece = HALF // BLOCKS
    to_i = []
    for at in range(BLOCKS):
        for n in range(piece):
            to_i.append((at // 2 * piece + n, at % 2 * LANES + HALF + at * piece + n))
    to_j = [(j, copy * HALF + j) for j in range(HALF) for copy in range(2)]
    return selection(2 * piece, 2 * LANES, to_i), selection(LANES, LANES, to_j)


def half_picks():
    count = HALF // 2
    to_i, to_j = [], []
    for odd in range(2):
        for n in range(count):
            to_i.append((n, odd * LANES + odd * HALF + count + n))
            to_j += [(odd * HALF + n, odd * LANES + copy * count + n) for copy in range(4)]
    return selection(count, 2 * LANES, to_i), selection(LANES, 2 * LANES, to_j)


def order_rows(traces, slots, kinds):
    rows, wins, samples = traces.shape
    tiles = samples // LANES
    piece = rows // BLOCKS
    step_wins = 16
    steps = wins // step_wins
    batch = 4
    used = max(kinds, key=len)
    pitch = len(used) * piece + 1

    def kernel(slots_ref, traces_ref, *refs):
        out_refs, (wide, in_ref, slot_ref, sems) = refs[:-4], refs[-4:]
        slot_copy = pltpu.make_async_copy(slots_ref, slot_ref, sems.at[steps])
        slot_copy.start()
        copies = []
        for step in range(steps):
            here = pl.ds(step * step_wins, step_wins)
            copies.append(
                pltpu.make_async_copy(traces_ref.at[:, here, :], in_ref.at[:, here, :], sems.at[step])
            )
            copies[-1].start()
        slot_copy.wait()
        z = lax.axis_index("chan")
        odd = lax.rem(z, 2)
        pair = jnp.where(z < 2, 2, 0)

        def some_windows(step):
            first_win = step * step_wins
            for at, position in enumerate(used):
                block = pair + position + (odd if position % 2 == 0 else -odd)
                first = lax.rem(block, BLOCKS) * piece

                def move(group, carry, at=at, first=first):
                    js = [group * batch + u for u in range(batch)]
                    picked = [
                        in_ref[slot_ref[first + j], pl.ds(first_win, step_wins), :].astype(jnp.float32) for j in js
                    ]
                    for j, row in zip(js, picked):
                        for tile in range(tiles):
                            wide[tile, pl.ds(at * piece + j, step_wins, stride=pitch), :] = row[
                                :, tile * LANES : (tile + 1) * LANES
                            ]
                    return carry

                lax.fori_loop(0, piece // batch, move, 0)

            def pack(w, carry):
                blocks = [
                    wide[tile, pl.ds(w * pitch, len(used) * piece), :].astype(jnp.bfloat16) for tile in range(tiles)
                ]
                for out_ref, kind in zip(out_refs, kinds):
                    first = used.index(kind[0]) * piece
                    for tile, block in enumerate(blocks):
                        out_ref[first_win + w, :, tile * LANES : (tile + 1) * LANES] = block[
                            first : first + len(kind) * piece
                        ]
                return carry

            lax.fori_loop(0, step_wins, pack, 0, unroll=2)

        for step in range(steps):
            copies[step].wait()
            some_windows(step)

    return kernel_call(
        kernel,
        "order_rows",
        0,
        3 * traces.size * 2,
        vmem_bytes=ORDER_VMEM_BYTES,
        out_shape=[jax.ShapeDtypeStruct((wins, len(kind) * piece, samples), jnp.bfloat16) for kind in kinds],
        in_specs=[pl.BlockSpec(memory_space=pltpu.HBM)] * 2,
        out_specs=[in_vmem()] * len(kinds),
        scratch_shapes=[
            pltpu.VMEM((tiles, (step_wins + 1) * pitch, LANES), jnp.float32),
            pltpu.VMEM(traces.shape, traces.dtype),
            pltpu.SMEM(slots.shape, slots.dtype),
            pltpu.SemaphoreType.DMA((steps + 1,)),
        ],
    )(slots, traces)


def diagonal(values, copies):
    blank = jnp.zeros_like(values)
    rows = [[values if at == copy else blank for at in range(copies)] for copy in range(copies)]
    return jnp.concatenate([jnp.concatenate(row, axis=1) for row in rows], axis=0)


def spectra(rows_j, rows_i, tables):
    wins, given, samples = rows_j.shape
    bins = samples // 2
    pairs = wins // 2
    depth = 2 * wins
    folded = HALF // given
    line = depth // folded
    pitch = line + 1
    per_step = 2 * folded
    batch = 8

    def kernel(j_ref, i_ref, table_ref, to_i_ref, to_j_ref, i_out, j_out, wide):
        same = lax.axis_index("sub") == lax.axis_index("rep")

        def spectrum_of(group):
            stacked = []
            for win in [per_step * group + u for u in range(per_step)]:
                here = j_ref[win]
                stacked += [here, jnp.where(same, here, i_ref[win])]
            wave = jnp.concatenate(stacked, axis=0)
            return lax.dot_general(table_ref[...], wave, NT, preferred_element_type=jnp.float32)

        def keep(group, spectrum):
            energy = jnp.sum(spectrum * spectrum, axis=0, keepdims=True) / bins
            white = spectrum * lax.rsqrt(energy + 1e-05)
            for half in range(2):
                for part in range(2):
                    if folded == 1:
                        row = half * wins + part * pairs + group
                    else:
                        row = part * pairs + 2 * group + half
                    wide[pl.ds(row, bins, stride=pitch), :] = white[
                        part * bins : (part + 1) * bins, half * LANES : (half + 1) * LANES
                    ]

        groups = wins // per_step
        at_once = 4

        def some_windows(step, carry):
            first = step * at_once
            last = spectrum_of(first)
            for group in range(1, at_once):
                now = spectrum_of(first + group)
                keep(first + group - 1, last)
                last = now
            keep(first + at_once - 1, last)
            return carry

        lax.fori_loop(0, groups // at_once, some_windows, 0)

        def moved(fs):
            loaded = [wide[pl.ds(f * pitch, line), :].astype(jnp.bfloat16) for f in fs]
            i_rows = [
                lax.dot_general(to_i_ref[...], diagonal(values, 2), NT, preferred_element_type=jnp.float32)
                for values in loaded
            ]
            if folded == 2:
                i_rows = [jnp.concatenate([rows[: given // 2], rows[given // 2 :]], axis=1) for rows in i_rows]
            j_rows = jnp.dot(jnp.concatenate(loaded, axis=0), to_j_ref[...], preferred_element_type=jnp.float32)
            return fs, i_rows, j_rows

        def store(fs, i_rows, j_rows):
            for at, f in enumerate(fs):
                i_out[f] = i_rows[at].astype(jnp.bfloat16)
                for odd in range(folded):
                    j_out[f, odd * line : (odd + 1) * line] = j_rows[
                        at * line : (at + 1) * line, odd * LANES : (odd + 1) * LANES
                    ].astype(jnp.bfloat16)

        def pack(group, carry):
            first = group * 4 * batch
            waiting = moved([first + u for u in range(batch)])
            for at in range(1, 4):
                following = moved([first + at * batch + u for u in range(batch)])
                store(*waiting)
                waiting = following
            store(*waiting)
            return carry

        lax.fori_loop(0, bins // (4 * batch), pack, 0)

    shapes = [(bins, given // 2, LANES), (bins, depth, LANES)]
    return kernel_call(
        kernel,
        "spectra",
        4 * samples * samples * wins * given,
        4 * wins * given * samples * 2,
        out_shape=[jax.ShapeDtypeStruct(shape, jnp.bfloat16) for shape in shapes],
        in_specs=[in_vmem()] * (2 + len(tables)),
        out_specs=[in_vmem()] * len(shapes),
        scratch_shapes=[pltpu.VMEM(((bins + 1) * pitch, LANES), jnp.float32)],
    )(rows_j, rows_i, *tables)


def partial_correlations(lefts, rights, tables, jobs, outs):
    left_arrays = [array for array, _ in lefts]
    right_arrays = [array for array, _, _ in rights]
    bins, depth, _ = right_arrays[0].shape
    piece = HALF // BLOCKS
    pitch = bins + 1
    step_bins = 32
    groups = []
    slices = {}
    for used, groups_here in jobs:
        js = [(rights[right][1], there) for right in used for there in rights[right][2]]
        for left, _, first in groups_here:
            found = []
            for offset in range(2):
                at = first + offset
                for order, (j_other, there) in enumerate(js):
                    if there != at:
                        kind = (lefts[left][1], j_other, there ^ (at % 2))
                        found.append((at, kind, offset * HALF + order * piece))
                        slices.setdefault(at, []).append(kind)
            groups.append(found)
    for kinds in slices.values():
        kinds.sort()
    total = len(groups) * piece
    batch = 4

    def first_of(at):
        (out,) = [positions for positions in outs if at in positions]
        return outs.index(out), sum(len(slices[before]) for before in out[: out.index(at)])

    def kernel(*refs):
        left_refs, rest = refs[: len(lefts)], refs[len(lefts) :]
        right_refs, rest = rest[: len(rights)], rest[len(rights) :]
        lag_ref, same_ref, out_refs, cross = rest[0], rest[1], rest[2:-1], rest[-1]
        lanes = lax.broadcasted_iota(jnp.int32, (depth, LANES), 1)

        first_half = lanes < HALF
        lower = lanes % HALF < HALF // 2
        blank = jnp.zeros((depth, LANES), jnp.bfloat16)

        def turn(values):
            swapped = []
            for first in range(0, depth, depth // 2):
                middle, last = first + depth // 4, first + depth // 2
                swapped += [-values[middle:last], values[first:middle]]
            return jnp.concatenate(swapped, axis=0)

        def right_hand(used, f):
            values = right_refs[used[0]][f]
            if len(used) == 2:
                values = jnp.where(lower, values, right_refs[used[1]][f])
            turned = turn(values)
            return jnp.concatenate(
                [
                    jnp.concatenate([jnp.where(first_half, part, blank) for part in (values, turned)], axis=1),
                    jnp.concatenate([jnp.where(first_half, blank, part) for part in (values, turned)], axis=1),
                ],
                axis=0,
            )

        def products(first_bin, count):
            found = []
            for f in [first_bin + u for u in range(count)]:
                first = 0
                for used, groups_here in jobs:
                    lhs = [left_refs[left][f, row : row + piece] for left, row, _ in groups_here]
                    lhs = jnp.concatenate(lhs, axis=0) if len(lhs) > 1 else lhs[0]
                    product = jnp.dot(lhs, right_hand(used, f), preferred_element_type=jnp.float32)
                    found.append((first * pitch + f, product))
                    first += lhs.shape[0]
            return found

        def keep(found):
            for here, product in found:
                for part in range(2):
                    cross[pl.ds(part * total * pitch + here, product.shape[0], stride=pitch), :] = product[
                        :, part * LANES : (part + 1) * LANES
                    ]

        def some_bins(step, carry):
            first = step * step_bins
            waiting = products(first, batch)
            for at in range(batch, step_bins, batch):
                following = products(first + at, batch)
                keep(waiting)
                waiting = following
            keep(waiting)
            return carry

        lax.fori_loop(0, bins // step_bins, some_bins, 0)

        for index, found in enumerate(groups):
            targets = []
            for at, kind, lane in found:
                out, first = first_of(at)
                targets.append((out_refs[out], first + slices[at].index(kind), lane))

            def summed(i):
                parts = []
                for part in range(2):
                    start = (part * total + index * piece + i) * pitch
                    parts.append(
                        jnp.concatenate([cross[pl.ds(start, bins), :], cross[pl.ds(start + pitch, bins), :]], axis=1)
                    )
                values = jnp.concatenate(parts, axis=0).astype(jnp.bfloat16)
                return i, jnp.dot(lag_ref[...], values, preferred_element_type=jnp.float32)

            def across(i, lagged):
                lagged = lagged.astype(jnp.bfloat16)
                return i, lax.dot_general(same_ref[...], lagged, NT, preferred_element_type=jnp.float32)

            def store(i, rows):
                for half in range(2):
                    for out, place, lane in targets:
                        row = half * LANES + lane
                        out[place, i + half] = rows[row : row + piece].astype(out.dtype)

            sums, rows = summed(0), None
            for i in range(2, piece, 2):
                more = summed(i)
                if rows is not None:
                    store(*rows)
                rows = across(*sums)
                sums = more
            store(*rows)
            store(*across(*sums))

    shapes = [(sum(len(slices[at]) for at in positions), piece, piece, LAGS) for positions in outs]
    types = [jnp.float32 if positions == (OWN_AT,) else jnp.bfloat16 for positions in outs]
    results = kernel_call(
        kernel,
        "partial_correlations",
        4 * total * bins * depth * LANES + 4 * total * bins * LANES * LAGS,
        2 * sum(array.size for array in left_arrays + right_arrays),
        out_shape=[jax.ShapeDtypeStruct(shape, kind) for shape, kind in zip(shapes, types)],
        in_specs=[in_vmem()] * (len(lefts) + len(rights) + len(tables)),
        out_specs=[in_vmem()] * len(shapes),
        scratch_shapes=[pltpu.VMEM(((2 * total + 1) * pitch, LANES), jnp.float32)],
    )(*left_arrays, *right_arrays, *tables)
    return results, slices


def assembled(shares):
    arrays = [array for array, _ in shares]
    _, piece, _, lags = arrays[0].shape
    width = 2 * piece

    def kernel(*refs):
        out, held, sems = refs[-3:]
        sub = lax.axis_index("sub")
        odd = lax.rem(lax.axis_index("chan"), 2)
        copies = []
        for there, round_at in ((0, 1), (1, 2 - 2 * odd), (3, 2 * odd)):
            for i_other in range(2):
                for j_other in range(2):
                    parts = [
                        refs[at][place].astype(jnp.float32)
                        for at, (_, kinds) in enumerate(shares)
                        for place, kind in enumerate(kinds)
                        if kind == (i_other, j_other, there)
                    ]
                    i_first = jnp.where(sub == 0, i_other, 1 - i_other) * piece
                    j_first = pl.multiple_of(jnp.where(sub == 0, j_other, 1 - j_other) * piece, piece)
                    held[round_at, 0, pl.ds(i_first, piece), pl.ds(j_first, piece), :] = functools.reduce(
                        jnp.add, parts
                    )
            at = len(copies)
            copies.append(pltpu.make_async_copy(held.at[round_at], out.at[round_at], sems.at[at]))
            copies[-1].start()
        for copy in copies:
            copy.wait()

    shape = (ROUNDS, 1, width, width, lags)
    return kernel_call(
        kernel,
        "assembled",
        0,
        sum(array.size for array in arrays) * 2,
        out_shape=jax.ShapeDtypeStruct(shape, jnp.float32),
        in_specs=[in_vmem()] * len(arrays),
        out_specs=pl.BlockSpec(memory_space=pl.ANY),
        scratch_shapes=[pltpu.VMEM(shape, jnp.float32), pltpu.SemaphoreType.DMA((ROUNDS,))],
    )(*arrays)


def summed_in_place(traces, channel_slot):
    chan_count = lax.axis_size("chan")
    _, win_here, samples = traces.shape
    piece = HALF // BLOCKS
    scale = (2.0 / (win_here * chan_count * (samples // 2))) ** 0.5
    dft_rows = dft_rows_table(samples)
    same = selection(2 * LANES, 2 * LANES, [(n, n) for n in range(2 * LANES)])
    tables = [lag_rows_table(samples, scale), same]
    everywhere = tuple(range(BLOCKS))

    def over_sub(rows):
        return lax.ppermute(rows, "sub", [(0, 1), (1, 0)])

    def over_core(rows):
        return lax.ppermute(rows, "rep", [(0, 1), (1, 0)])

    def with_device(share, apart):
        return lax.ppermute(share, "chan", [(z, z ^ apart) for z in range(chan_count)])

    def after(value, *others):
        return lax.optimization_barrier((value,) + others)[0]

    def added(share, arrived):
        return (share.astype(jnp.float32) + arrived.astype(jnp.float32)).astype(jnp.bfloat16)

    def for_two_away(kinds):
        return [(i_other, j_other, there ^ 2) for i_other, j_other, there in kinds]

    mine, mine_far, mine_near = order_rows(traces, channel_slot, [everywhere, FAR, NEAR])
    far = over_sub(mine_far)
    near = over_sub(mine_near)

    own_i, own_j = spectra(mine, over_core(mine), (dft_rows, *own_picks()))
    own_left, own_right = (own_i, 0), (own_j, 0, everywhere)
    own_far, own_near = (0, 0, FAR[0]), (0, piece, NEAR[0])
    (kept_1, own_1, sent_1), kinds_1 = partial_correlations(
        [own_left], [own_right], tables, [((0,), [own_far, own_near])], [(0,), (2,), (1, 3)]
    )
    arrived_1 = with_device(sent_1, 1)

    far = after(far, kept_1, own_1, sent_1)
    far_i, far_j = spectra(far, over_core(far), (dft_rows, *half_picks()))
    far_left, far_right = (far_i, 1), (far_j, 1, FAR)
    other_far = (1, 0, FAR[0])
    (kept_2, sent_far_2, own_2, sent_near_2), kinds_2 = partial_correlations(
        [own_left, far_left],
        [own_right, far_right],
        tables,
        [((0,), [other_far]), ((1,), [own_far, own_near, other_far])],
        [(0,), (1,), (2,), (3,)],
    )
    arrived_far_2 = with_device(sent_far_2, 1)

    near, arrived_far_2, arrived_1 = lax.optimization_barrier((near, arrived_far_2, arrived_1))
    near_i, near_j = spectra(near, over_core(near), (dft_rows, *half_picks()))
    summed_2 = added(kept_2, arrived_far_2)
    far_2 = with_device(summed_2, 2)
    far_count_1 = kept_1.shape[0]
    summed_1 = added(after(kept_1, near_j), arrived_1[:far_count_1])
    far_1 = with_device(summed_1, 2)
    near_j = after(near_j, summed_2)
    near_left, near_right = (near_i, 1), (near_j, 1, NEAR)
    (kept_3, sent_far_3, own_3, sent_near_3), kinds_3 = partial_correlations(
        [own_left, far_left],
        [near_right],
        tables,
        [((0,), [own_far, other_far, own_near])],
        [(0,), (1,), (2,), (3,)],
    )
    arrived_far_3 = with_device(sent_far_3, 1)
    arrived_near_2 = with_device(sent_near_2, 1)
    near_right = (after(near_j, kept_3, sent_far_3, far_2, summed_1, arrived_near_2), 1, NEAR)
    (own_4, sent_4), kinds_4 = partial_correlations(
        [near_left], [far_right, near_right], tables, [((0, 1), [(0, 0, NEAR[0])])], [(2,), (3,)]
    )
    arrived_4 = with_device(jnp.concatenate([sent_near_3, sent_4]), 1)
    summed_3 = added(after(kept_3, own_4), arrived_far_3)
    far_3 = with_device(summed_3, 2)
    near_left = (after(near_i, own_4, sent_4, summed_3, far_1), 1)
    (own_5, sent_5), kinds_5 = partial_correlations(
        [near_left], [own_right], tables, [((0,), [(0, 0, NEAR[0])])], [(2,), (3,)]
    )
    arrived_5 = with_device(sent_5, 1)
    shares = [
        (own_1, kinds_1[2]),
        (own_2, kinds_2[2]),
        (own_3, kinds_3[2]),
        (own_4, kinds_4[2]),
        (own_5, kinds_5[2]),
        (arrived_1, [None] * far_count_1 + kinds_1[3]),
        (arrived_near_2, kinds_2[3]),
        (arrived_4, kinds_3[3] + kinds_4[3]),
        (arrived_5, kinds_5[3]),
        (far_1, for_two_away(kinds_1[0])),
        (far_2, for_two_away(kinds_2[0])),
        (far_3, for_two_away(kinds_3[0])),
    ]
    return assembled(shares)


def from_behind(shard, axis, by):
    count = lax.axis_size(axis)
    return lax.ppermute(shard, axis, [(i, (i + by) % count) for i in range(count)])


def dft_columns(samples, parts, sub_bins):
    shape = (samples, parts, 2, sub_bins)
    time_pos = lax.broadcasted_iota(jnp.int32, shape, 0)
    range_pos = lax.broadcasted_iota(jnp.int32, shape, 1)
    part_pos = lax.broadcasted_iota(jnp.int32, shape, 2)
    bin_pos = lax.broadcasted_iota(jnp.int32, shape, 3)
    frequency = range_pos * sub_bins + bin_pos
    angles = jnp.mod(time_pos * frequency, samples).astype(jnp.float32) * (2.0 * math.pi / samples)
    entries = jnp.where(part_pos == 0, jnp.cos(angles), -jnp.sin(angles))
    return entries.reshape(samples, parts * 2 * sub_bins).astype(jnp.bfloat16)


def lag_table(sub_bins, first_bin, lag_count, samples):
    frequency = first_bin + lax.broadcasted_iota(jnp.int32, (sub_bins, lag_count), 0)
    lag_offset = lax.broadcasted_iota(jnp.int32, (sub_bins, lag_count), 1) - lag_count // 2
    angles = jnp.mod(frequency * lag_offset, samples).astype(jnp.float32) * (2.0 * math.pi / samples)
    return jnp.stack([jnp.cos(angles), -jnp.sin(angles)], axis=1)


def moved_spectra(traces, channel_slot):
    chan_count = lax.axis_size("chan")
    sub_count = lax.axis_size("sub")
    group_rows, win_here, samples = traces.shape
    bin_count = samples // 2
    sub_bins = bin_count // sub_count
    bin_width = 2 * sub_bins
    piece_len = group_rows // chan_count
    picked = jnp.take(traces, channel_slot, axis=0)
    dft_rows = dft_columns(samples, sub_count, sub_bins)
    spectrum = jnp.dot(picked.reshape(-1, samples), dft_rows, preferred_element_type=jnp.float32)
    energy = jnp.sum(spectrum * spectrum, axis=1, keepdims=True) / bin_count
    whitened = (spectrum * lax.rsqrt(energy + 1e-05)).astype(jnp.bfloat16)
    whitened = whitened.reshape(chan_count, piece_len, win_here, sub_count, bin_width)
    regrouped = lax.all_to_all(whitened, "chan", split_axis=0, concat_axis=0, tiled=True)
    regrouped = lax.all_to_all(regrouped, "sub", split_axis=3, concat_axis=3, tiled=True)
    own_half = regrouped.transpose(3, 1, 0, 2, 4).reshape(sub_count * piece_len, chan_count * win_here, bin_width)
    own_block = lax.all_gather(own_half, "rep", axis=0, tiled=True)
    windows = own_block.shape[1]
    own_split = own_block.reshape(own_block.shape[0], windows, 2, sub_bins)
    lag_rows = lag_table(sub_bins, lax.axis_index("sub") * sub_bins, LAGS, samples)
    lag_scale = (2.0 / (windows * bin_count)) ** 0.5
    results = []
    for step in range(1, ROUNDS + 1):
        partner = from_behind(own_half, "chan", -step)
        partner_split = partner.reshape(partner.shape[0], windows, 2, sub_bins)
        turned = jnp.stack([-partner_split[:, :, 1], partner_split[:, :, 0]], axis=2)
        partner_pair = jnp.stack([partner_split, turned], axis=0)
        cross_spec = jnp.einsum("iwpf,qjwpf->fqij", own_split, partner_pair, preferred_element_type=jnp.float32)
        summed = jnp.einsum("fqij,fql->ijl", cross_spec, lag_rows, precision=lax.Precision.HIGHEST)
        results.append(lax.psum_scatter(lag_scale * summed, "sub", scatter_dimension=0, tiled=True))
    return jnp.stack(results)[:, None]


def solution(mesh):
    sizes = mesh.shape
    in_place = sizes["chan"] == BLOCKS == ROUNDS + 1 and sizes["sub"] == 2 and sizes["rep"] == 2
    return jax.shard_map(
        summed_in_place if in_place else moved_spectra,
        mesh=mesh,
        in_specs=(P(("groups", "sub", "rep"), "chan", None), P(("groups", "sub", "rep"))),
        out_specs=P(None, ("groups", "chan"), "sub", "rep", None),
        check_vma=False,
    )
```

profile of v0, /device:TPU:0, one launch (start us, length us, event | category | flops | bytes accessed | tf_op | source)
XLA Modules:
  0.0 103.8 jit_solution(9184698322903736342)
XLA Ops:
  0.7 2.3 %order_rows.1 = (bf16[32,64,512]{2,1,0:T(8,128)(2,1)S(1)}, bf16[32,32,512]{2,1,0:T(8,128)(2,1)S(1)}, bf16[32,32,512]{2,1,0:T(8,128)(2,1)S(1)}) custom-call(s32[64]{0:T(128)S(1)} %copy-done.2, bf16[64,32,512]{2,1,0:T(8,128)(2,1)} %traces_ref.1), custom_call_target="tpu_custom_call" | custom-call | bytes 6291456 | tf_op jit(solution)/shard_map/order_rows/pallas_call | solution.py:147
  3.5 2.6 %collective-permute-start.1 = (bf16[32,32,512]{2,1,0:T(8,128)(2,1)S(1)}, bf16[32,32,512]{2,1,0:T(8,128)(2,1)S(1)}, u32[]{:S(2)}, u32[]{:S(2)}) collective-permute-start(bf16[32,32,512]{2,1,0:T(8,128)(2,1)S(1)} %get-tuple-element.42), channel_id=1, source_target_pairs={{0,2},{2,0},{1,3},{3,1},{4,6},{6,4},{5,7},{7,5},{8,10},{10,8},{9,1... | collective-permute-start | bytes 3145736 | tf_op jit(solution)/shard_map/ppermute | solution.py:461
  7.3 10.5 %spectra.3 = (bf16[256,32,128]{2,1,0:T(8,128)(2,1)S(1)}, bf16[256,64,128]{2,1,0:T(8,128)(2,1)S(1)}) custom-call(bf16[32,64,512]{2,1,0:T(8,128)(2,1)S(1)} %get-tuple-element.38.j_ref, bf16[32,64,512]{2,1,0:T(8,128)(2,1)S(1)} %collective-permute-done.i_ref, bf16[512,512]{1,0:T(8,128)(2,1)S(1)} %copy-done.3, bf16[32,256]{1,0:T(8,128)(2,1)S(1)} %copy-done.7, ...), custom_call_target="tpu_custom_call" | custom-call | flops 2147483648 | bytes 8388608 | tf_op jit(solution)/shard_map/spectra/pallas_call | solution.py:253
  17.8 4.8 %partial_correlations.5 = (bf16[3,16,16,128]{3,2,1,0:T(8,128)(2,1)S(1)}, f32[3,16,16,128]{3,2,1,0:T(8,128)S(1)}, bf16[6,16,16,128]{3,2,1,0:T(8,128)(2,1)S(1)}) custom-call(bf16[256,32,128]{2,1,0:T(8,128)(2,1)S(1)} %get-tuple-element.39.refs_0_, bf16[256,64,128]{2,1,0:T(8,128)(2,1)S(1)} %get-tuple-element.40.refs_1_.refs_2_, bf16[128,512]{1,0:T(8,128)(2,1)S(1)} %copy-done.1, ...), custom_call_target="tpu_custom_call" | custom-call | flops 805306368 | bytes 6291456 | tf_op jit(solution)/shard_map/partial_correlations/pallas_call | solution.py:394
  22.6 7.2 %collective-permute-done.1.j_ref = bf16[32,32,512]{2,1,0:T(8,128)(2,1)S(1)} collective-permute-done((bf16[32,32,512]{2,1,0:T(8,128)(2,1)S(1)}, bf16[32,32,512]{2,1,0:T(8,128)(2,1)S(1)}, u32[]{:S(2)}, u32[]{:S(2)}) %collective-permute-start.1) | collective-permute-done | bytes 1048608 | tf_op jit(solution)/shard_map/ppermute | solution.py:461
  29.8 1.8 %collective-permute-start.3 = (bf16[32,32,512]{2,1,0:T(8,128)(2,1)S(1)}, bf16[32,32,512]{2,1,0:T(8,128)(2,1)S(1)}, u32[]{:S(2)}, u32[]{:S(2)}) collective-permute-start(bf16[32,32,512]{2,1,0:T(8,128)(2,1)S(1)} %get-tuple-element.49), channel_id=1, source_target_pairs={{0,2},{2,0},{1,3},{3,1},{4,6},{6,4},{5,7},{7,5},{8,10},{10,8},{9,1... | collective-permute-start | bytes 3145736 | tf_op jit(solution)/shard_map/ppermute | solution.py:461
  31.6 1.6 %collective-permute-start.5 = (bf16[6,16,16,128]{3,2,1,0:T(8,128)(2,1)S(1)}, bf16[6,16,16,128]{3,2,1,0:T(8,128)(2,1)S(1)}, u32[]{:S(2)}, u32[]{:S(2)}) collective-permute-start(bf16[6,16,16,128]{3,2,1,0:T(8,128)(2,1)S(1)} %get-tuple-element.44), channel_id=1, source_target_pairs={{0,4},{4,0},{8,12},{12,8},{1,5},{5,1},{9,13},{13,9},{2,6},{6,2},{1... | collective-permute-start | bytes 1179656 | tf_op jit(solution)/shard_map/ppermute | solution.py:467
  33.1 6.8 %spectra.4 = (bf16[256,16,128]{2,1,0:T(8,128)(2,1)S(1)}, bf16[256,64,128]{2,1,0:T(8,128)(2,1)S(1)}) custom-call(bf16[32,32,512]{2,1,0:T(8,128)(2,1)S(1)} %collective-permute-done.1.j_ref, bf16[32,32,512]{2,1,0:T(8,128)(2,1)S(1)} %collective-permute-done.2.i_ref, bf16[512,512]{1,0:T(8,128)(2,1)S(1)} %copy-done.3, bf16[32,256]{1,0:T(8,128)(2,1)S(1)} %copy-done.6, ...), custom_call_target="tpu_custom_call" | custom-call | flops 1073741824 | bytes 4194304 | tf_op jit(solution)/shard_map/spectra/pallas_call | solution.py:253
  39.9 8.3 %partial_correlations.6 = (bf16[5,16,16,128]{3,2,1,0:T(8,128)(2,1)S(1)}, bf16[5,16,16,128]{3,2,1,0:T(8,128)(2,1)S(1)}, f32[2,16,16,128]{3,2,1,0:T(8,128)S(1)}, bf16[2,16,16,128]{3,2,1,0:T(8,128)(2,1)S(1)}) custom-call(bf16[256,32,128]{2,1,0:T(8,128)(2,1)S(1)} %get-tuple-element.39.refs_0_, bf16[256,16,128]{2,1,0:T(8,128)(2,1)S(1)} %get-tuple-element.46.refs_1_, ...), custom_call_target="tpu_custom_call" | custom-call | flops 1610612736 | bytes 11534336 | tf_op jit(solution)/shard_map/partial_correlations/pallas_call | solution.py:394
  48.2 1.2 %collective-permute-start.4 = (bf16[5,16,16,128]{3,2,1,0:T(8,128)(2,1)S(1)}, bf16[5,16,16,128]{3,2,1,0:T(8,128)(2,1)S(1)}, u32[]{:S(2)}, u32[]{:S(2)}) collective-permute-start(bf16[5,16,16,128]{3,2,1,0:T(8,128)(2,1)S(1)} %get-tuple-element.50), channel_id=1, source_target_pairs={{0,4},{4,0},{8,12},{12,8},{1,5},{5,1},{9,13},{13,9},{2,6},{6,2},{1... | collective-permute-start | bytes 983048 | tf_op jit(solution)/shard_map/ppermute | solution.py:467
  49.4 6.0 %collective-permute-done.3.j_ref = bf16[32,32,512]{2,1,0:T(8,128)(2,1)S(1)} collective-permute-done((bf16[32,32,512]{2,1,0:T(8,128)(2,1)S(1)}, bf16[32,32,512]{2,1,0:T(8,128)(2,1)S(1)}, u32[]{:S(2)}, u32[]{:S(2)}) %collective-permute-start.3) | collective-permute-done | bytes 1048608 | tf_op jit(solution)/shard_map/ppermute | solution.py:461
  55.4 2.4 %collective-permute-done.4 = bf16[5,16,16,128]{3,2,1,0:T(8,128)(2,1)S(1)} collective-permute-done((bf16[5,16,16,128]{3,2,1,0:T(8,128)(2,1)S(1)}, bf16[5,16,16,128]{3,2,1,0:T(8,128)(2,1)S(1)}, u32[]{:S(2)}, u32[]{:S(2)}) %collective-permute-start.4) | collective-permute-done | bytes 327712 | tf_op jit(solution)/shard_map/ppermute | solution.py:467
  57.8 1.3 %collective-permute-start.8 = (bf16[2,16,16,128]{3,2,1,0:T(8,128)(2,1)S(1)}, bf16[2,16,16,128]{3,2,1,0:T(8,128)(2,1)S(1)}, u32[]{:S(2)}, u32[]{:S(2)}) collective-permute-start(bf16[2,16,16,128]{3,2,1,0:T(8,128)(2,1)S(1)} %get-tuple-element.62), channel_id=1, source_target_pairs={{0,4},{4,0},{8,12},{12,8},{1,5},{5,1},{9,13},{13,9},{2,6},{6,2},{1... | collective-permute-start | bytes 393224 | tf_op jit(solution)/shard_map/ppermute | solution.py:467
  59.3 2.7 %collective-permute-start.7 = (bf16[5,16,16,128]{3,2,1,0:T(8,128)(2,1)S(1)}, bf16[5,16,16,128]{3,2,1,0:T(8,128)(2,1)S(1)}, u32[]{:S(2)}, u32[]{:S(2)}) collective-permute-start(bf16[5,16,16,128]{3,2,1,0:T(8,128)(2,1)S(1)} %add_convert_fusion), channel_id=1, source_target_pairs={{0,8},{4,12},{8,0},{12,4},{1,9},{5,13},{9,1},{13,5},{2,10},{6,14},... | collective-permute-start | bytes 983048 | tf_op jit(solution)/shard_map/ppermute | solution.py:467
  61.9 6.7 %spectra.5 = (bf16[256,16,128]{2,1,0:T(8,128)(2,1)S(1)}, bf16[256,64,128]{2,1,0:T(8,128)(2,1)S(1)}) custom-call(bf16[32,32,512]{2,1,0:T(8,128)(2,1)S(1)} %collective-permute-done.3.j_ref, bf16[32,32,512]{2,1,0:T(8,128)(2,1)S(1)} %collective-permute-done.6.i_ref, bf16[512,512]{1,0:T(8,128)(2,1)S(1)} %copy-done.3, bf16[32,256]{1,0:T(8,128)(2,1)S(1)} %copy-done.6, ...), custom_call_target="tpu_custom_call" | custom-call | flops 1073741824 | bytes 4194304 | tf_op jit(solution)/shard_map/spectra/pallas_call | solution.py:253
  68.7 5.7 %partial_correlations.7 = (bf16[4,16,16,128]{3,2,1,0:T(8,128)(2,1)S(1)}, bf16[4,16,16,128]{3,2,1,0:T(8,128)(2,1)S(1)}, f32[1,16,16,128]{3,2,1,0:T(8,128)S(1)}, bf16[1,16,16,128]{3,2,1,0:T(8,128)(2,1)S(1)}) custom-call(bf16[256,32,128]{2,1,0:T(8,128)(2,1)S(1)} %get-tuple-element.39.refs_0_, bf16[256,16,128]{2,1,0:T(8,128)(2,1)S(1)} %get-tuple-element.46.refs_1_, ...), custom_call_target="tpu_custom_call" | custom-call | flops 1207959552 | bytes 7340032 | tf_op jit(solution)/shard_map/partial_correlations/pallas_call | solution.py:394
  75.2 1.9 %collective-permute-start.10 = (bf16[3,16,16,128]{3,2,1,0:T(8,128)(2,1)S(1)}, bf16[3,16,16,128]{3,2,1,0:T(8,128)(2,1)S(1)}, u32[]{:S(2)}, u32[]{:S(2)}) collective-permute-start(bf16[3,16,16,128]{3,2,1,0:T(8,128)(2,1)S(1)} %add_convert_fusion.2), channel_id=1, source_target_pairs={{0,8},{4,12},{8,0},{12,4},{1,9},{5,13},{9,1},{13,5},{2,10},{6,14},... | collective-permute-start | bytes 589832 | tf_op jit(solution)/shard_map/ppermute | solution.py:467
  77.1 4.0 %partial_correlations.8 = (f32[3,16,16,128]{3,2,1,0:T(8,128)S(1)}, bf16[3,16,16,128]{3,2,1,0:T(8,128)(2,1)S(1)}) custom-call(bf16[256,16,128]{2,1,0:T(8,128)(2,1)S(1)} %get-tuple-element.67.refs_0_, bf16[256,64,128]{2,1,0:T(8,128)(2,1)S(1)} %get-tuple-element.47.refs_3_.refs_1_, bf16[256,64,128]{2,1,0:T(8,128)(2,1)S(1)} %get-tuple-element.63.refs_2_, ...), custom_call_target="tpu_custom_call" | custom-call | flops 402653184 | bytes 9437184 | tf_op jit(solution)/shard_map/partial_correlations/pallas_call | solution.py:394
  81.9 6.0 %collective-permute-done.9 = bf16[4,16,16,128]{3,2,1,0:T(8,128)(2,1)S(1)} collective-permute-done((bf16[4,16,16,128]{3,2,1,0:T(8,128)(2,1)S(1)}, bf16[4,16,16,128]{3,2,1,0:T(8,128)(2,1)S(1)}, u32[]{:S(2)}, u32[]{:S(2)}) %collective-permute-start.9) | collective-permute-done | bytes 262176 | tf_op jit(solution)/shard_map/ppermute | solution.py:467
  88.0 4.0 %partial_correlations.9 = (f32[3,16,16,128]{3,2,1,0:T(8,128)S(1)}, bf16[3,16,16,128]{3,2,1,0:T(8,128)(2,1)S(1)}) custom-call(bf16[256,16,128]{2,1,0:T(8,128)(2,1)S(1)} %get-tuple-element.67.refs_0_, bf16[256,64,128]{2,1,0:T(8,128)(2,1)S(1)} %get-tuple-element.40.refs_1_.refs_2_, bf16[128,512]{1,0:T(8,128)(2,1)S(1)} %copy-done.1, bf16[256,256]{1,0:T(8,128)(2,1)S(1)} %copy-done), custom_call_target="tpu_custom_call" | custom-call | flops 402653184 | bytes 5242880 | tf_op jit(solution)/shard_map/partial_correlations/pallas_call | solution.py:394
  92.0 2.5 %collective-permute-start.12 = (bf16[3,16,16,128]{3,2,1,0:T(8,128)(2,1)S(1)}, bf16[3,16,16,128]{3,2,1,0:T(8,128)(2,1)S(1)}, u32[]{:S(2)}, u32[]{:S(2)}) collective-permute-start(bf16[3,16,16,128]{3,2,1,0:T(8,128)(2,1)S(1)} %get-tuple-element.70), channel_id=1, source_target_pairs={{0,4},{4,0},{8,12},{12,8},{1,5},{5,1},{9,13},{13,9},{2,6},{6,2},{1... | collective-permute-start | bytes 589832 | tf_op jit(solution)/shard_map/ppermute | solution.py:467
  94.6 2.4 %collective-permute-done.11.refs_7_ = bf16[4,16,16,128]{3,2,1,0:T(8,128)(2,1)S(1)} collective-permute-done((bf16[4,16,16,128]{3,2,1,0:T(8,128)(2,1)S(1)}, bf16[4,16,16,128]{3,2,1,0:T(8,128)(2,1)S(1)}, u32[]{:S(2)}, u32[]{:S(2)}) %collective-permute-start.11) | collective-permute-done | bytes 262176 | tf_op jit(solution)/shard_map/ppermute | solution.py:467
  96.9 5.5 %collective-permute-done.12.refs_8_ = bf16[3,16,16,128]{3,2,1,0:T(8,128)(2,1)S(1)} collective-permute-done((bf16[3,16,16,128]{3,2,1,0:T(8,128)(2,1)S(1)}, bf16[3,16,16,128]{3,2,1,0:T(8,128)(2,1)S(1)}, u32[]{:S(2)}, u32[]{:S(2)}) %collective-permute-start.12) | collective-permute-done | bytes 196640 | tf_op jit(solution)/shard_map/ppermute | solution.py:467
  102.4 1.2 %assembled.1 = f32[3,1,32,32,128]{4,3,2,1,0:T(8,128)} custom-call(f32[3,16,16,128]{3,2,1,0:T(8,128)S(1)} %get-tuple-element.41.refs_0_, f32[2,16,16,128]{3,2,1,0:T(8,128)S(1)} %get-tuple-element.48.refs_1_, f32[1,16,16,128]{3,2,1,0:T(8,128)S(1)} %get-tuple-element.56.refs_2_, f32[3,16,16,128]{3,2,1,0:T(8,128)S(1)} %get-tuple-element.64.refs_3_, ...), custom_call_target="tpu_custom_call" | custom-call | bytes 2555904 | tf_op jit(solution)/shard_map/assembled/pallas_call | solution.py:438
  (34 shorter events, 4.3 us)
Async XLA Ops:
  0.0 0.7 copy-start.2
  0.7 6.6 %copy-start.3 = (bf16[512,512]{1,0:T(8,128)(2,1)S(1)}, bf16[512,512]{1,0:T(8,128)(2,1)}, u32[]{:S(2)}) copy-start(bf16[512,512]{1,0:T(8,128)(2,1)} %constant.21.table_ref) | copy-start | bytes 1572868
  0.7 6.6 %copy-start.5 = (bf16[128,128]{1,0:T(8,128)(2,1)S(1)}, bf16[128,128]{1,0:T(8,128)(2,1)}, u32[]{:S(2)}) copy-start(bf16[128,128]{1,0:T(8,128)(2,1)} %constant.23.to_j_ref) | copy-start | bytes 98308
  0.7 6.6 %copy-start.7 = (bf16[32,256]{1,0:T(8,128)(2,1)S(1)}, bf16[32,256]{1,0:T(8,128)(2,1)}, u32[]{:S(2)}) copy-start(bf16[32,256]{1,0:T(8,128)(2,1)} %constant.22.to_i_ref) | copy-start | bytes 49156
  2.9 4.3 %collective-permute-start = (bf16[32,64,512]{2,1,0:T(8,128)(2,1)S(1)}, bf16[32,64,512]{2,1,0:T(8,128)(2,1)S(1)}, u32[]{:S(2)}, u32[]{:S(2)}) collective-permute-start(bf16[32,64,512]{2,1,0:T(8,128)(2,1)S(1)} %get-tuple-element.38.j_ref), channel_id=1, source_target_pairs={{0,1},{1,0},{2,3},{3,2},{4,5},{5,4},{6,7},{7,6},{8,9},{9,8},{10,11... | collective-permute-start | bytes 6291464 | tf_op jit(solution)/shard_map/ppermute | solution.py:464
  3.5 14.3 %copy-start = (bf16[256,256]{1,0:T(8,128)(2,1)S(1)}, bf16[256,256]{1,0:T(8,128)(2,1)}, u32[]{:S(2)}) copy-start(bf16[256,256]{1,0:T(8,128)(2,1)} %constant.25.refs_3_.refs_5_.refs_4_) | copy-start | bytes 393220
  3.5 14.3 %copy-start.1 = (bf16[128,512]{1,0:T(8,128)(2,1)S(1)}, bf16[128,512]{1,0:T(8,128)(2,1)}, u32[]{:S(2)}) copy-start(bf16[128,512]{1,0:T(8,128)(2,1)} %constant.24.refs_2_.refs_4_.refs_3_) | copy-start | bytes 393220
  3.5 26.3 %collective-permute-start.1 = (bf16[32,32,512]{2,1,0:T(8,128)(2,1)S(1)}, bf16[32,32,512]{2,1,0:T(8,128)(2,1)S(1)}, u32[]{:S(2)}, u32[]{:S(2)}) collective-permute-start(bf16[32,32,512]{2,1,0:T(8,128)(2,1)S(1)} %get-tuple-element.42), channel_id=1, source_target_pairs={{0,2},{2,0},{1,3},{3,1},{4,6},{6,4},{5,7},{7,5},{8,10},{10,8},{9,1... | collective-permute-start | bytes 3145736 | tf_op jit(solution)/shard_map/ppermute | solution.py:461
  17.7 15.4 %copy-start.4 = (bf16[128,256]{1,0:T(8,128)(2,1)S(1)}, bf16[128,256]{1,0:T(8,128)(2,1)}, u32[]{:S(2)}) copy-start(bf16[128,256]{1,0:T(8,128)(2,1)} %constant.27.to_j_ref) | copy-start | bytes 196612
  17.8 15.4 %copy-start.6 = (bf16[32,256]{1,0:T(8,128)(2,1)S(1)}, bf16[32,256]{1,0:T(8,128)(2,1)}, u32[]{:S(2)}) copy-start(bf16[32,256]{1,0:T(8,128)(2,1)} %constant.26.to_i_ref) | copy-start | bytes 49156
  29.8 3.3 %collective-permute-start.2 = (bf16[32,32,512]{2,1,0:T(8,128)(2,1)S(1)}, bf16[32,32,512]{2,1,0:T(8,128)(2,1)S(1)}, u32[]{:S(2)}, u32[]{:S(2)}) collective-permute-start(bf16[32,32,512]{2,1,0:T(8,128)(2,1)S(1)} %collective-permute-done.1.j_ref), channel_id=1, source_target_pairs={{0,1},{1,0},{2,3},{3,2},{4,5},{5,4},{6,7},{7,6},{8,9},{9,8},{10,11... | collective-permute-start | bytes 3145736 | tf_op jit(solution)/shard_map/ppermute | solution.py:464
  29.8 25.6 %collective-permute-start.3 = (bf16[32,32,512]{2,1,0:T(8,128)(2,1)S(1)}, bf16[32,32,512]{2,1,0:T(8,128)(2,1)S(1)}, u32[]{:S(2)}, u32[]{:S(2)}) collective-permute-start(bf16[32,32,512]{2,1,0:T(8,128)(2,1)S(1)} %get-tuple-element.49), channel_id=1, source_target_pairs={{0,2},{2,0},{1,3},{3,1},{4,6},{6,4},{5,7},{7,5},{8,10},{10,8},{9,1... | collective-permute-start | bytes 3145736 | tf_op jit(solution)/shard_map/ppermute | solution.py:461
  31.6 23.8 %collective-permute-start.5 = (bf16[6,16,16,128]{3,2,1,0:T(8,128)(2,1)S(1)}, bf16[6,16,16,128]{3,2,1,0:T(8,128)(2,1)S(1)}, u32[]{:S(2)}, u32[]{:S(2)}) collective-permute-start(bf16[6,16,16,128]{3,2,1,0:T(8,128)(2,1)S(1)} %get-tuple-element.44), channel_id=1, source_target_pairs={{0,4},{4,0},{8,12},{12,8},{1,5},{5,1},{9,13},{13,9},{2,6},{6,2},{1... | collective-permute-start | bytes 1179656 | tf_op jit(solution)/shard_map/ppermute | solution.py:467
  48.2 9.6 %collective-permute-start.4 = (bf16[5,16,16,128]{3,2,1,0:T(8,128)(2,1)S(1)}, bf16[5,16,16,128]{3,2,1,0:T(8,128)(2,1)S(1)}, u32[]{:S(2)}, u32[]{:S(2)}) collective-permute-start(bf16[5,16,16,128]{3,2,1,0:T(8,128)(2,1)S(1)} %get-tuple-element.50), channel_id=1, source_target_pairs={{0,4},{4,0},{8,12},{12,8},{1,5},{5,1},{9,13},{13,9},{2,6},{6,2},{1... | collective-permute-start | bytes 983048 | tf_op jit(solution)/shard_map/ppermute | solution.py:467
  57.8 4.1 %collective-permute-start.6 = (bf16[32,32,512]{2,1,0:T(8,128)(2,1)S(1)}, bf16[32,32,512]{2,1,0:T(8,128)(2,1)S(1)}, u32[]{:S(2)}, u32[]{:S(2)}) collective-permute-start(bf16[32,32,512]{2,1,0:T(8,128)(2,1)S(1)} %collective-permute-done.3.j_ref), channel_id=1, source_target_pairs={{0,1},{1,0},{2,3},{3,2},{4,5},{5,4},{6,7},{7,6},{8,9},{9,8},{10,11... | collective-permute-start | bytes 3145736 | tf_op jit(solution)/shard_map/ppermute | solution.py:464
  57.8 19.2 %collective-permute-start.8 = (bf16[2,16,16,128]{3,2,1,0:T(8,128)(2,1)S(1)}, bf16[2,16,16,128]{3,2,1,0:T(8,128)(2,1)S(1)}, u32[]{:S(2)}, u32[]{:S(2)}) collective-permute-start(bf16[2,16,16,128]{3,2,1,0:T(8,128)(2,1)S(1)} %get-tuple-element.62), channel_id=1, source_target_pairs={{0,4},{4,0},{8,12},{12,8},{1,5},{5,1},{9,13},{13,9},{2,6},{6,2},{1... | collective-permute-start | bytes 393224 | tf_op jit(solution)/shard_map/ppermute | solution.py:467
  59.3 17.9 %collective-permute-start.7 = (bf16[5,16,16,128]{3,2,1,0:T(8,128)(2,1)S(1)}, bf16[5,16,16,128]{3,2,1,0:T(8,128)(2,1)S(1)}, u32[]{:S(2)}, u32[]{:S(2)}) collective-permute-start(bf16[5,16,16,128]{3,2,1,0:T(8,128)(2,1)S(1)} %add_convert_fusion), channel_id=1, source_target_pairs={{0,8},{4,12},{8,0},{12,4},{1,9},{5,13},{9,1},{13,5},{2,10},{6,14},... | collective-permute-start | bytes 983048 | tf_op jit(solution)/shard_map/ppermute | solution.py:467
  74.4 13.5 %collective-permute-start.9 = (bf16[4,16,16,128]{3,2,1,0:T(8,128)(2,1)S(1)}, bf16[4,16,16,128]{3,2,1,0:T(8,128)(2,1)S(1)}, u32[]{:S(2)}, u32[]{:S(2)}) collective-permute-start(bf16[4,16,16,128]{3,2,1,0:T(8,128)(2,1)S(1)} %get-tuple-element.59), channel_id=1, source_target_pairs={{0,4},{4,0},{8,12},{12,8},{1,5},{5,1},{9,13},{13,9},{2,6},{6,2},{1... | collective-permute-start | bytes 786440 | tf_op jit(solution)/shard_map/ppermute | solution.py:467
  75.2 12.8 %collective-permute-start.10 = (bf16[3,16,16,128]{3,2,1,0:T(8,128)(2,1)S(1)}, bf16[3,16,16,128]{3,2,1,0:T(8,128)(2,1)S(1)}, u32[]{:S(2)}, u32[]{:S(2)}) collective-permute-start(bf16[3,16,16,128]{3,2,1,0:T(8,128)(2,1)S(1)} %add_convert_fusion.2), channel_id=1, source_target_pairs={{0,8},{4,12},{8,0},{12,4},{1,9},{5,13},{9,1},{13,5},{2,10},{6,14},... | collective-permute-start | bytes 589832 | tf_op jit(solution)/shard_map/ppermute | solution.py:467
  81.2 15.7 %collective-permute-start.11 = (bf16[4,16,16,128]{3,2,1,0:T(8,128)(2,1)S(1)}, bf16[4,16,16,128]{3,2,1,0:T(8,128)(2,1)S(1)}, u32[]{:S(2)}, u32[]{:S(2)}) collective-permute-start(bf16[4,16,16,128]{3,2,1,0:T(8,128)(2,1)S(1)} %pad_maximum_fusion), channel_id=1, source_target_pairs={{0,4},{4,0},{8,12},{12,8},{1,5},{5,1},{9,13},{13,9},{2,6},{6,2},{1... | collective-permute-start | bytes 786440 | tf_op jit(solution)/shard_map/ppermute | solution.py:467
  87.9 14.5 %collective-permute-start.13 = (bf16[4,16,16,128]{3,2,1,0:T(8,128)(2,1)S(1)}, bf16[4,16,16,128]{3,2,1,0:T(8,128)(2,1)S(1)}, u32[]{:S(2)}, u32[]{:S(2)}) collective-permute-start(bf16[4,16,16,128]{3,2,1,0:T(8,128)(2,1)S(1)} %add_convert_fusion.1), channel_id=1, source_target_pairs={{0,8},{4,12},{8,0},{12,4},{1,9},{5,13},{9,1},{13,5},{2,10},{6,14},... | collective-permute-start | bytes 786440 | tf_op jit(solution)/shard_map/ppermute | solution.py:467
  92.0 10.4 %collective-permute-start.12 = (bf16[3,16,16,128]{3,2,1,0:T(8,128)(2,1)S(1)}, bf16[3,16,16,128]{3,2,1,0:T(8,128)(2,1)S(1)}, u32[]{:S(2)}, u32[]{:S(2)}) collective-permute-start(bf16[3,16,16,128]{3,2,1,0:T(8,128)(2,1)S(1)} %get-tuple-element.70), channel_id=1, source_target_pairs={{0,4},{4,0},{8,12},{12,8},{1,5},{5,1},{9,13},{13,9},{2,6},{6,2},{1... | collective-permute-start | bytes 589832 | tf_op jit(solution)/shard_map/ppermute | solution.py:467
where the time goes:
time: 104 us
  Pallas kernels  54.3 us (52%)
  waiting for transfers between devices  30.7 us (30%)
  starting transfers between devices  17.6 us (17%)
    pallas_call x5, Pallas kernels, partial_correlations(): kernel_call(kernel, 'partial_correlations', 4 * total * bins * depth * LA...  26.8 us
    pallas_call x3, Pallas kernels, spectra(): kernel_call(kernel, 'spectra', 4 * samples * samples * wins * given, 4 *...  24 us
    ppermute x9, waiting for transfers between devices, with_device(): lax.ppermute(share, 'chan', [(z, z ^ apart) for z in range(chan_count)])  16.3 us
    ppermute x2, waiting for transfers between devices, over_sub(): return lax.ppermute(rows, 'sub', [(0, 1), (1, 0)])  13.2 us
    ppermute x9, starting transfers between devices, with_device(): lax.ppermute(share, 'chan', [(z, z ^ apart) for z in range(chan_count)])  12.7 us
    ppermute x2, starting transfers between devices, over_sub(): return lax.ppermute(rows, 'sub', [(0, 1), (1, 0)])  4.35 us
    pallas_call x1, Pallas kernels, order_rows(): kernel_call(kernel, 'order_rows', 0, 3 * traces.size * 2, vmem_bytes=ORDE...  2.28 us
  transfers between devices with their start and end apart: 14, of which 8 were waited for; matrix products, arithmetic and copies ran while one was open for 0% of the time, Pallas kernels for 49%

commit v1 on v0

--- a/solution.py
+++ b/solution.py
@@ -168,7 +168,7 @@
     return jnp.concatenate([jnp.concatenate(row, axis=1) for row in rows], axis=0)
 
 
-def spectra(rows_j, rows_i, tables):
+def spectra_steps(rows_j):
     wins, given, samples = rows_j.shape
     bins = samples // 2
     pairs = wins // 2
@@ -179,7 +179,7 @@
     per_step = 2 * folded
     batch = 8
 
-    def kernel(j_ref, i_ref, table_ref, to_i_ref, to_j_ref, i_out, j_out, wide):
+    def run(j_ref, i_ref, table_ref, to_i_ref, to_j_ref, i_out, j_out, wide):
         same = lax.axis_index("sub") == lax.axis_index("rep")
 
         def spectrum_of(group):
@@ -250,22 +250,27 @@
         lax.fori_loop(0, bins // (4 * batch), pack, 0)
 
     shapes = [(bins, given // 2, LANES), (bins, depth, LANES)]
+    outs = [jax.ShapeDtypeStruct(shape, jnp.bfloat16) for shape in shapes]
+    scratch = [pltpu.VMEM(((bins + 1) * pitch, LANES), jnp.float32)]
+    return run, outs, scratch, 4 * samples * samples * wins * given
+
+
+def spectra(rows_j, rows_i, tables):
+    run, outs, scratch, flops = spectra_steps(rows_j)
     return kernel_call(
-        kernel,
+        run,
         "spectra",
-        4 * samples * samples * wins * given,
-        4 * wins * given * samples * 2,
-        out_shape=[jax.ShapeDtypeStruct(shape, jnp.bfloat16) for shape in shapes],
+        flops,
+        8 * rows_j.size,
+        out_shape=outs,
         in_specs=[in_vmem()] * (2 + len(tables)),
-        out_specs=[in_vmem()] * len(shapes),
-        scratch_shapes=[pltpu.VMEM(((bins + 1) * pitch, LANES), jnp.float32)],
+        out_specs=[in_vmem()] * len(outs),
+        scratch_shapes=scratch,
     )(rows_j, rows_i, *tables)
 
 
-def partial_correlations(lefts, rights, tables, jobs, outs):
-    left_arrays = [array for array, _ in lefts]
-    right_arrays = [array for array, _, _ in rights]
-    bins, depth, _ = right_arrays[0].shape
+def correlation_steps(lefts, rights, jobs, outs):
+    bins, depth, _ = rights[0][0].shape
     piece = HALF // BLOCKS
     pitch = bins + 1
     step_bins = 32
@@ -292,10 +297,7 @@
         (out,) = [positions for positions in outs if at in positions]
         return outs.index(out), sum(len(slices[before]) for before in out[: out.index(at)])
 
-    def kernel(*refs):
-        left_refs, rest = refs[: len(lefts)], refs[len(lefts) :]
-        right_refs, rest = rest[: len(rights)], rest[len(rights) :]
-        lag_ref, same_ref, out_refs, cross = rest[0], rest[1], rest[2:-1], rest[-1]
+    def run(left_refs, right_refs, lag_ref, same_ref, out_refs, cross):
         lanes = lax.broadcasted_iota(jnp.int32, (depth, LANES), 1)
 
         first_half = lanes < HALF
@@ -391,17 +393,61 @@
 
     shapes = [(sum(len(slices[at]) for at in positions), piece, piece, LAGS) for positions in outs]
     types = [jnp.float32 if positions == (OWN_AT,) else jnp.bfloat16 for positions in outs]
+    out_shapes = [jax.ShapeDtypeStruct(shape, kind) for shape, kind in zip(shapes, types)]
+    scratch = [pltpu.VMEM(((2 * total + 1) * pitch, LANES), jnp.float32)]
+    return run, out_shapes, scratch, 4 * total * bins * (depth + LAGS) * LANES, slices
+
+
+def partial_correlations(lefts, rights, tables, jobs, outs):
+    run, out_shapes, scratch, flops, slices = correlation_steps(lefts, rights, jobs, outs)
+    arrays = [left[0] for left in lefts] + [right[0] for right in rights]
+
+    def kernel(*refs):
+        left_refs, rest = refs[: len(lefts)], refs[len(lefts) :]
+        right_refs, rest = rest[: len(rights)], rest[len(rights) :]
+        run(left_refs, right_refs, rest[0], rest[1], rest[2:-1], rest[-1])
+
     results = kernel_call(
         kernel,
         "partial_correlations",
-        4 * total * bins * depth * LANES + 4 * total * bins * LANES * LAGS,
-        2 * sum(array.size for array in left_arrays + right_arrays),
-        out_shape=[jax.ShapeDtypeStruct(shape, kind) for shape, kind in zip(shapes, types)],
-        in_specs=[in_vmem()] * (len(lefts) + len(rights) + len(tables)),
-        out_specs=[in_vmem()] * len(shapes),
-        scratch_shapes=[pltpu.VMEM(((2 * total + 1) * pitch, LANES), jnp.float32)],
-    )(*left_arrays, *right_arrays, *tables)
+        flops,
+        2 * sum(array.size for array in arrays),
+        out_shape=out_shapes,
+        in_specs=[in_vmem()] * (len(arrays) + len(tables)),
+        out_specs=[in_vmem()] * len(out_shapes),
+        scratch_shapes=scratch,
+    )(*arrays, *tables)
     return results, slices
+
+
+def spectra_and_correlations(rows_j, rows_i, spectra_tables, js, lefts, rights, tables, jobs, outs):
+    run_spectra, spectra_outs, spectra_scratch, spectra_flops = spectra_steps(rows_j)
+    run, out_shapes, scratch, flops, slices = correlation_steps(
+        lefts + [(spectra_outs[0], 1)], rights + [(spectra_outs[1], 1, js)], jobs, outs
+    )
+    given = [rows_j, rows_i, *spectra_tables]
+    arrays = [left[0] for left in lefts] + [right[0] for right in rights]
+    last_right = len(given) + len(arrays)
+
+    def kernel(*refs):
+        left_refs = refs[len(given) : len(given) + len(lefts)]
+        right_refs = refs[len(given) + len(lefts) : last_right]
+        lag_ref, same_ref, i_out, j_out = refs[last_right : last_right + 4]
+        out_refs, (wide, cross) = refs[last_right + 4 : -2], refs[-2:]
+        run_spectra(*refs[: len(given)], i_out, j_out, wide)
+        run([*left_refs, i_out], [*right_refs, j_out], lag_ref, same_ref, out_refs, cross)
+
+    results = kernel_call(
+        kernel,
+        "spectra_and_correlations",
+        spectra_flops + flops,
+        8 * rows_j.size,
+        out_shape=spectra_outs + out_shapes,
+        in_specs=[in_vmem()] * (last_right + len(tables)),
+        out_specs=[in_vmem()] * (2 + len(out_shapes)),
+        scratch_shapes=spectra_scratch + scratch,
+    )(*given, *arrays, *tables)
+    return results[0], results[1], results[2:], slices
 
 
 def assembled(shares):
@@ -488,34 +534,39 @@
     arrived_1 = with_device(sent_1, 1)
 
     far = after(far, kept_1, own_1, sent_1)
-    far_i, far_j = spectra(far, over_core(far), (dft_rows, *half_picks()))
+    far_i, far_j, (kept_2, sent_far_2, own_2, sent_near_2), kinds_2 = spectra_and_correlations(
+        far,
+        over_core(far),
+        (dft_rows, *half_picks()),
+        FAR,
+        [own_left],
+        [own_right],
+        tables,
+        [((0,), [(1, 0, FAR[0])]), ((1,), [own_far, own_near, (1, 0, FAR[0])])],
+        [(0,), (1,), (2,), (3,)],
+    )
     far_left, far_right = (far_i, 1), (far_j, 1, FAR)
-    other_far = (1, 0, FAR[0])
-    (kept_2, sent_far_2, own_2, sent_near_2), kinds_2 = partial_correlations(
-        [own_left, far_left],
-        [own_right, far_right],
-        tables,
-        [((0,), [other_far]), ((1,), [own_far, own_near, other_far])],
-        [(0,), (1,), (2,), (3,)],
-    )
     arrived_far_2 = with_device(sent_far_2, 1)
 
     near, arrived_far_2, arrived_1 = lax.optimization_barrier((near, arrived_far_2, arrived_1))
-    near_i, near_j = spectra(near, over_core(near), (dft_rows, *half_picks()))
+    near_core = over_core(near)
     summed_2 = added(kept_2, arrived_far_2)
     far_2 = with_device(summed_2, 2)
+    near_i, near_j, (kept_3, sent_far_3, own_3, sent_near_3), kinds_3 = spectra_and_correlations(
+        after(near, summed_2),
+        near_core,
+        (dft_rows, *half_picks()),
+        NEAR,
+        [own_left, far_left],
+        [],
+        tables,
+        [((0,), [own_far, (1, 0, FAR[0]), own_near])],
+        [(0,), (1,), (2,), (3,)],
+    )
+    near_left, near_right = (near_i, 1), (near_j, 1, NEAR)
     far_count_1 = kept_1.shape[0]
-    summed_1 = added(after(kept_1, near_j), arrived_1[:far_count_1])
+    summed_1 = added(after(kept_1, kept_3), arrived_1[:far_count_1])
     far_1 = with_device(summed_1, 2)
-    near_j = after(near_j, summed_2)
-    near_left, near_right = (near_i, 1), (near_j, 1, NEAR)
-    (kept_3, sent_far_3, own_3, sent_near_3), kinds_3 = partial_correlations(
-        [own_left, far_left],
-        [near_right],
-        tables,
-        [((0,), [own_far, other_far, own_near])],
-        [(0,), (1,), (2,), (3,)],
-    )
     arrived_far_3 = with_device(sent_far_3, 1)
     arrived_near_2 = with_device(sent_near_2, 1)
     near_right = (after(near_j, kept_3, sent_far_3, far_2, summed_1, arrived_near_2), 1, NEAR)

time: 104 us -> 104 us (level)
    pallas_call x8 -> x6, Pallas kernels: 50.8 us -> 50.8 us  [the longest x2 27.5 us: spectra_and_correlations(): kernel_call(kernel, 'spectra_and_correlations', spectra_flops + flops, 8...]
where the time goes in v1:
time: 104 us
  Pallas kernels  54.3 us (52%)
  waiting for transfers between devices  30.7 us (30%)
  starting transfers between devices  17.7 us (17%)
    pallas_call x2, Pallas kernels, spectra_and_correlations(): kernel_call(kernel, 'spectra_and_correlations', spectra_flops + flops, 8...  27.5 us
    ppermute x9, waiting for transfers between devices, with_device(): lax.ppermute(share, 'chan', [(z, z ^ apart) for z in range(chan_count)])  16.3 us
    ppermute x2, waiting for transfers between devices, over_sub(): return lax.ppermute(rows, 'sub', [(0, 1), (1, 0)])  13.2 us
    pallas_call x3, Pallas kernels, partial_correlations(): kernel_call(kernel, 'partial_correlations', flops, 2 * sum((array.size fo...  12.8 us
    ppermute x9, starting transfers between devices, with_device(): lax.ppermute(share, 'chan', [(z, z ^ apart) for z in range(chan_count)])  12.8 us
    pallas_call x1, Pallas kernels, spectra(): kernel_call(run, 'spectra', flops, 8 * rows_j.size, out_shape=outs, in_sp...  10.5 us
    ppermute x2, starting transfers between devices, over_sub(): return lax.ppermute(rows, 'sub', [(0, 1), (1, 0)])  4.35 us
    pallas_call x1, Pallas kernels, order_rows(): kernel_call(kernel, 'order_rows', 0, 3 * traces.size * 2, vmem_bytes=ORDE...  2.28 us
  transfers between devices with their start and end apart: 14, of which 8 were waited for; matrix products, arithmetic and copies ran while one was open for 0% of the time, Pallas kernels for 49%

profile of v1, /device:TPU:0, one launch (start us, length us, event | category | flops | bytes accessed | tf_op | source)
XLA Modules:
  0.0 103.8 jit_solution(13170299983486850163)
XLA Ops:
  0.7 2.3 %order_rows.1 = (bf16[32,64,512]{2,1,0:T(8,128)(2,1)S(1)}, bf16[32,32,512]{2,1,0:T(8,128)(2,1)S(1)}, bf16[32,32,512]{2,1,0:T(8,128)(2,1)S(1)}) custom-call(s32[64]{0:T(128)S(1)} %copy-done.2, bf16[64,32,512]{2,1,0:T(8,128)(2,1)} %traces_ref.1), custom_call_target="tpu_custom_call" | custom-call | bytes 6291456 | tf_op jit(solution)/shard_map/order_rows/pallas_call | solution.py:147
  3.5 2.6 %collective-permute-start.1 = (bf16[32,32,512]{2,1,0:T(8,128)(2,1)S(1)}, bf16[32,32,512]{2,1,0:T(8,128)(2,1)S(1)}, u32[]{:S(2)}, u32[]{:S(2)}) collective-permute-start(bf16[32,32,512]{2,1,0:T(8,128)(2,1)S(1)} %get-tuple-element.42), channel_id=1, source_target_pairs={{0,2},{2,0},{1,3},{3,1},{4,6},{6,4},{5,7},{7,5},{8,10},{10,8},{9,1... | collective-permute-start | bytes 3145736 | tf_op jit(solution)/shard_map/ppermute | solution.py:507
  6.1 1.2 %collective-permute-done.i_ref = bf16[32,64,512]{2,1,0:T(8,128)(2,1)S(1)} collective-permute-done((bf16[32,64,512]{2,1,0:T(8,128)(2,1)S(1)}, bf16[32,64,512]{2,1,0:T(8,128)(2,1)S(1)}, u32[]{:S(2)}, u32[]{:S(2)}) %collective-permute-start) | collective-permute-done | bytes 2097184 | tf_op jit(solution)/shard_map/ppermute | solution.py:510
  7.3 10.5 %spectra.1 = (bf16[256,32,128]{2,1,0:T(8,128)(2,1)S(1)}, bf16[256,64,128]{2,1,0:T(8,128)(2,1)S(1)}) custom-call(bf16[32,64,512]{2,1,0:T(8,128)(2,1)S(1)} %get-tuple-element.38.j_ref, bf16[32,64,512]{2,1,0:T(8,128)(2,1)S(1)} %collective-permute-done.i_ref, bf16[512,512]{1,0:T(8,128)(2,1)S(1)} %copy-done.3, bf16[32,256]{1,0:T(8,128)(2,1)S(1)} %copy-done.7, ...), custom_call_target="tpu_custom_call" | custom-call | flops 2147483648 | bytes 8388608 | tf_op jit(solution)/shard_map/spectra/pallas_call | solution.py:260
  17.8 4.8 %partial_correlations.3 = (bf16[3,16,16,128]{3,2,1,0:T(8,128)(2,1)S(1)}, f32[3,16,16,128]{3,2,1,0:T(8,128)S(1)}, bf16[6,16,16,128]{3,2,1,0:T(8,128)(2,1)S(1)}) custom-call(bf16[256,32,128]{2,1,0:T(8,128)(2,1)S(1)} %get-tuple-element.39.refs_0_.refs_5_, bf16[256,64,128]{2,1,0:T(8,128)(2,1)S(1)} %get-tuple-element.40.refs_1_.refs_6_, ...), custom_call_target="tpu_custom_call" | custom-call | flops 805306368 | bytes 6291456 | tf_op jit(solution)/shard_map/partial_correlations/pallas_call | solution.py:410
  22.6 7.2 %collective-permute-done.1.refs_0_ = bf16[32,32,512]{2,1,0:T(8,128)(2,1)S(1)} collective-permute-done((bf16[32,32,512]{2,1,0:T(8,128)(2,1)S(1)}, bf16[32,32,512]{2,1,0:T(8,128)(2,1)S(1)}, u32[]{:S(2)}, u32[]{:S(2)}) %collective-permute-start.1) | collective-permute-done | bytes 1048608 | tf_op jit(solution)/shard_map/ppermute | solution.py:507
  29.8 1.8 %collective-permute-start.3 = (bf16[32,32,512]{2,1,0:T(8,128)(2,1)S(1)}, bf16[32,32,512]{2,1,0:T(8,128)(2,1)S(1)}, u32[]{:S(2)}, u32[]{:S(2)}) collective-permute-start(bf16[32,32,512]{2,1,0:T(8,128)(2,1)S(1)} %get-tuple-element.47), channel_id=1, source_target_pairs={{0,2},{2,0},{1,3},{3,1},{4,6},{6,4},{5,7},{7,5},{8,10},{10,8},{9,1... | collective-permute-start | bytes 3145736 | tf_op jit(solution)/shard_map/ppermute | solution.py:507
  31.6 1.6 %collective-permute-start.5 = (bf16[6,16,16,128]{3,2,1,0:T(8,128)(2,1)S(1)}, bf16[6,16,16,128]{3,2,1,0:T(8,128)(2,1)S(1)}, u32[]{:S(2)}, u32[]{:S(2)}) collective-permute-start(bf16[6,16,16,128]{3,2,1,0:T(8,128)(2,1)S(1)} %get-tuple-element.44), channel_id=1, source_target_pairs={{0,4},{4,0},{8,12},{12,8},{1,5},{5,1},{9,13},{13,9},{2,6},{6,2},{1... | collective-permute-start | bytes 1179656 | tf_op jit(solution)/shard_map/ppermute | solution.py:513
  33.1 15.0 %spectra_and_correlations.2 = (bf16[256,16,128]{2,1,0:T(8,128)(2,1)S(1)}, bf16[256,64,128]{2,1,0:T(8,128)(2,1)S(1)}, bf16[5,16,16,128]{3,2,1,0:T(8,128)(2,1)S(1)...) custom-call(bf16[32,32,512]{2,1,0:T(8,128)(2,1)S(1)} %collective-permut, ...), custom_call_target="tpu_custom_call" | custom-call | flops 2684354560 | bytes 4194304 | tf_op jit(solution)/shard_map/spectra_and_correlations/pallas_call | solution.py:440
  48.2 1.2 %collective-permute-start.4 = (bf16[5,16,16,128]{3,2,1,0:T(8,128)(2,1)S(1)}, bf16[5,16,16,128]{3,2,1,0:T(8,128)(2,1)S(1)}, u32[]{:S(2)}, u32[]{:S(2)}) collective-permute-start(bf16[5,16,16,128]{3,2,1,0:T(8,128)(2,1)S(1)} %get-tuple-element.48), channel_id=1, source_target_pairs={{0,4},{4,0},{8,12},{12,8},{1,5},{5,1},{9,13},{13,9},{2,6},{6,2},{1... | collective-permute-start | bytes 983048 | tf_op jit(solution)/shard_map/ppermute | solution.py:513
  49.4 6.0 %collective-permute-done.3.refs_0_ = bf16[32,32,512]{2,1,0:T(8,128)(2,1)S(1)} collective-permute-done((bf16[32,32,512]{2,1,0:T(8,128)(2,1)S(1)}, bf16[32,32,512]{2,1,0:T(8,128)(2,1)S(1)}, u32[]{:S(2)}, u32[]{:S(2)}) %collective-permute-start.3) | collective-permute-done | bytes 1048608 | tf_op jit(solution)/shard_map/ppermute | solution.py:507
  55.4 2.4 %collective-permute-done.4 = bf16[5,16,16,128]{3,2,1,0:T(8,128)(2,1)S(1)} collective-permute-done((bf16[5,16,16,128]{3,2,1,0:T(8,128)(2,1)S(1)}, bf16[5,16,16,128]{3,2,1,0:T(8,128)(2,1)S(1)}, u32[]{:S(2)}, u32[]{:S(2)}) %collective-permute-start.4) | collective-permute-done | bytes 327712 | tf_op jit(solution)/shard_map/ppermute | solution.py:513
  57.8 1.3 %collective-permute-start.8 = (bf16[2,16,16,128]{3,2,1,0:T(8,128)(2,1)S(1)}, bf16[2,16,16,128]{3,2,1,0:T(8,128)(2,1)S(1)}, u32[]{:S(2)}, u32[]{:S(2)}) collective-permute-start(bf16[2,16,16,128]{3,2,1,0:T(8,128)(2,1)S(1)} %get-tuple-element.62), channel_id=1, source_target_pairs={{0,4},{4,0},{8,12},{12,8},{1,5},{5,1},{9,13},{13,9},{2,6},{6,2},{1... | collective-permute-start | bytes 393224 | tf_op jit(solution)/shard_map/ppermute | solution.py:513
  59.3 2.7 %collective-permute-start.7 = (bf16[5,16,16,128]{3,2,1,0:T(8,128)(2,1)S(1)}, bf16[5,16,16,128]{3,2,1,0:T(8,128)(2,1)S(1)}, u32[]{:S(2)}, u32[]{:S(2)}) collective-permute-start(bf16[5,16,16,128]{3,2,1,0:T(8,128)(2,1)S(1)} %add_convert_fusion), channel_id=1, source_target_pairs={{0,8},{4,12},{8,0},{12,4},{1,9},{5,13},{9,1},{13,5},{2,10},{6,14},... | collective-permute-start | bytes 983048 | tf_op jit(solution)/shard_map/ppermute | solution.py:513
  61.9 12.5 %spectra_and_correlations.3 = (bf16[256,16,128]{2,1,0:T(8,128)(2,1)S(1)}, bf16[256,64,128]{2,1,0:T(8,128)(2,1)S(1)}, bf16[4,16,16,128]{3,2,1,0:T(8,128)(2,1)S(1)...) custom-call(bf16[32,32,512]{2,1,0:T(8,128)(2,1)S(1)} %collective-permut, ...), custom_call_target="tpu_custom_call" | custom-call | flops 2281701376 | bytes 4194304 | tf_op jit(solution)/shard_map/spectra_and_correlations/pallas_call | solution.py:440
  74.4 0.8 collective-permute-start.9
  75.2 1.9 %collective-permute-start.10 = (bf16[3,16,16,128]{3,2,1,0:T(8,128)(2,1)S(1)}, bf16[3,16,16,128]{3,2,1,0:T(8,128)(2,1)S(1)}, u32[]{:S(2)}, u32[]{:S(2)}) collective-permute-start(bf16[3,16,16,128]{3,2,1,0:T(8,128)(2,1)S(1)} %add_convert_fusion.2), channel_id=1, source_target_pairs={{0,8},{4,12},{8,0},{12,4},{1,9},{5,13},{9,1},{13,5},{2,10},{6,14},... | collective-permute-start | bytes 589832 | tf_op jit(solution)/shard_map/ppermute | solution.py:513
  77.1 4.0 %partial_correlations.4 = (f32[3,16,16,128]{3,2,1,0:T(8,128)S(1)}, bf16[3,16,16,128]{3,2,1,0:T(8,128)(2,1)S(1)}) custom-call(bf16[256,16,128]{2,1,0:T(8,128)(2,1)S(1)} %get-tuple-element.67.refs_0_, bf16[256,64,128]{2,1,0:T(8,128)(2,1)S(1)} %get-tuple-element.56.refs_1_, bf16[256,64,128]{2,1,0:T(8,128)(2,1)S(1)} %get-tuple-element.63.refs_2_, ...), custom_call_target="tpu_custom_call" | custom-call | flops 402653184 | bytes 9437184 | tf_op jit(solution)/shard_map/partial_correlations/pallas_call | solution.py:410
  81.9 5.9 %collective-permute-done.9 = bf16[4,16,16,128]{3,2,1,0:T(8,128)(2,1)S(1)} collective-permute-done((bf16[4,16,16,128]{3,2,1,0:T(8,128)(2,1)S(1)}, bf16[4,16,16,128]{3,2,1,0:T(8,128)(2,1)S(1)}, u32[]{:S(2)}, u32[]{:S(2)}) %collective-permute-start.9) | collective-permute-done | bytes 262176 | tf_op jit(solution)/shard_map/ppermute | solution.py:513
  88.0 4.0 %partial_correlations.5 = (f32[3,16,16,128]{3,2,1,0:T(8,128)S(1)}, bf16[3,16,16,128]{3,2,1,0:T(8,128)(2,1)S(1)}) custom-call(bf16[256,16,128]{2,1,0:T(8,128)(2,1)S(1)} %get-tuple-element.67.refs_0_, bf16[256,64,128]{2,1,0:T(8,128)(2,1)S(1)} %get-tuple-element.40.refs_1_.refs_6_, bf16[128,512]{1,0:T(8,128)(2,1)S(1)} %copy-done.1, bf16[256,256]{1,0:T(8,128)(2,1)S(1)} %copy-done), custom_call_target="tpu_custom_call" | custom-call | flops 402653184 | bytes 5242880 | tf_op jit(solution)/shard_map/partial_correlations/pallas_call | solution.py:410
  92.0 2.6 %collective-permute-start.12 = (bf16[3,16,16,128]{3,2,1,0:T(8,128)(2,1)S(1)}, bf16[3,16,16,128]{3,2,1,0:T(8,128)(2,1)S(1)}, u32[]{:S(2)}, u32[]{:S(2)}) collective-permute-start(bf16[3,16,16,128]{3,2,1,0:T(8,128)(2,1)S(1)} %get-tuple-element.70), channel_id=1, source_target_pairs={{0,4},{4,0},{8,12},{12,8},{1,5},{5,1},{9,13},{13,9},{2,6},{6,2},{1... | collective-permute-start | bytes 589832 | tf_op jit(solution)/shard_map/ppermute | solution.py:513
  94.6 2.4 %collective-permute-done.11.refs_7_ = bf16[4,16,16,128]{3,2,1,0:T(8,128)(2,1)S(1)} collective-permute-done((bf16[4,16,16,128]{3,2,1,0:T(8,128)(2,1)S(1)}, bf16[4,16,16,128]{3,2,1,0:T(8,128)(2,1)S(1)}, u32[]{:S(2)}, u32[]{:S(2)}) %collective-permute-start.11) | collective-permute-done | bytes 262176 | tf_op jit(solution)/shard_map/ppermute | solution.py:513
  96.9 5.5 %collective-permute-done.12.refs_8_ = bf16[3,16,16,128]{3,2,1,0:T(8,128)(2,1)S(1)} collective-permute-done((bf16[3,16,16,128]{3,2,1,0:T(8,128)(2,1)S(1)}, bf16[3,16,16,128]{3,2,1,0:T(8,128)(2,1)S(1)}, u32[]{:S(2)}, u32[]{:S(2)}) %collective-permute-start.12) | collective-permute-done | bytes 196640 | tf_op jit(solution)/shard_map/ppermute | solution.py:513
  102.4 1.2 %assembled.1 = f32[3,1,32,32,128]{4,3,2,1,0:T(8,128)} custom-call(f32[3,16,16,128]{3,2,1,0:T(8,128)S(1)} %get-tuple-element.41.refs_0_, f32[2,16,16,128]{3,2,1,0:T(8,128)S(1)} %get-tuple-element.46.refs_1_, f32[1,16,16,128]{3,2,1,0:T(8,128)S(1)} %get-tuple-element.54.refs_2_, f32[3,16,16,128]{3,2,1,0:T(8,128)S(1)} %get-tuple-element.64.refs_3_, ...), custom_call_target="tpu_custom_call" | custom-call | bytes 2555904 | tf_op jit(solution)/shard_map/assembled/pallas_call | solution.py:484
  (32 shorter events, 2.3 us)
Async XLA Ops:
  0.0 0.7 copy-start.2
  0.7 6.6 %copy-start.3 = (bf16[512,512]{1,0:T(8,128)(2,1)S(1)}, bf16[512,512]{1,0:T(8,128)(2,1)}, u32[]{:S(2)}) copy-start(bf16[512,512]{1,0:T(8,128)(2,1)} %constant.21.table_ref.refs_2_) | copy-start | bytes 1572868
  0.7 6.6 %copy-start.5 = (bf16[128,128]{1,0:T(8,128)(2,1)S(1)}, bf16[128,128]{1,0:T(8,128)(2,1)}, u32[]{:S(2)}) copy-start(bf16[128,128]{1,0:T(8,128)(2,1)} %constant.23.to_j_ref) | copy-start | bytes 98308
  0.7 6.6 %copy-start.7 = (bf16[32,256]{1,0:T(8,128)(2,1)S(1)}, bf16[32,256]{1,0:T(8,128)(2,1)}, u32[]{:S(2)}) copy-start(bf16[32,256]{1,0:T(8,128)(2,1)} %constant.22.to_i_ref) | copy-start | bytes 49156
  2.9 4.3 %collective-permute-start = (bf16[32,64,512]{2,1,0:T(8,128)(2,1)S(1)}, bf16[32,64,512]{2,1,0:T(8,128)(2,1)S(1)}, u32[]{:S(2)}, u32[]{:S(2)}) collective-permute-start(bf16[32,64,512]{2,1,0:T(8,128)(2,1)S(1)} %get-tuple-element.38.j_ref), channel_id=1, source_target_pairs={{0,1},{1,0},{2,3},{3,2},{4,5},{5,4},{6,7},{7,6},{8,9},{9,8},{10,11... | collective-permute-start | bytes 6291464 | tf_op jit(solution)/shard_map/ppermute | solution.py:510
  3.5 14.3 %copy-start = (bf16[256,256]{1,0:T(8,128)(2,1)S(1)}, bf16[256,256]{1,0:T(8,128)(2,1)}, u32[]{:S(2)}) copy-start(bf16[256,256]{1,0:T(8,128)(2,1)} %constant.25.refs_3_.refs_8_.refs_4_) | copy-start | bytes 393220
  3.5 14.3 %copy-start.1 = (bf16[128,512]{1,0:T(8,128)(2,1)S(1)}, bf16[128,512]{1,0:T(8,128)(2,1)}, u32[]{:S(2)}) copy-start(bf16[128,512]{1,0:T(8,128)(2,1)} %constant.24.refs_2_.refs_7_.refs_3_) | copy-start | bytes 393220
  3.5 26.3 %collective-permute-start.1 = (bf16[32,32,512]{2,1,0:T(8,128)(2,1)S(1)}, bf16[32,32,512]{2,1,0:T(8,128)(2,1)S(1)}, u32[]{:S(2)}, u32[]{:S(2)}) collective-permute-start(bf16[32,32,512]{2,1,0:T(8,128)(2,1)S(1)} %get-tuple-element.42), channel_id=1, source_target_pairs={{0,2},{2,0},{1,3},{3,1},{4,6},{6,4},{5,7},{7,5},{8,10},{10,8},{9,1... | collective-permute-start | bytes 3145736 | tf_op jit(solution)/shard_map/ppermute | solution.py:507
  17.7 15.4 %copy-start.4 = (bf16[128,256]{1,0:T(8,128)(2,1)S(1)}, bf16[128,256]{1,0:T(8,128)(2,1)}, u32[]{:S(2)}) copy-start(bf16[128,256]{1,0:T(8,128)(2,1)} %constant.27.refs_4_) | copy-start | bytes 196612
  17.8 15.4 %copy-start.6 = (bf16[32,256]{1,0:T(8,128)(2,1)S(1)}, bf16[32,256]{1,0:T(8,128)(2,1)}, u32[]{:S(2)}) copy-start(bf16[32,256]{1,0:T(8,128)(2,1)} %constant.26.refs_3_) | copy-start | bytes 49156
  29.8 3.3 %collective-permute-start.2 = (bf16[32,32,512]{2,1,0:T(8,128)(2,1)S(1)}, bf16[32,32,512]{2,1,0:T(8,128)(2,1)S(1)}, u32[]{:S(2)}, u32[]{:S(2)}) collective-permute-start(bf16[32,32,512]{2,1,0:T(8,128)(2,1)S(1)} %collective-permute-done.1.refs_0_), channel_id=1, source_target_pairs={{0,1},{1,0},{2,3},{3,2},{4,5},{5,4},{6,7},{7,6},{8,9},{9,8},{10,11... | collective-permute-start | bytes 3145736 | tf_op jit(solution)/shard_map/ppermute | solution.py:510
  29.8 25.6 %collective-permute-start.3 = (bf16[32,32,512]{2,1,0:T(8,128)(2,1)S(1)}, bf16[32,32,512]{2,1,0:T(8,128)(2,1)S(1)}, u32[]{:S(2)}, u32[]{:S(2)}) collective-permute-start(bf16[32,32,512]{2,1,0:T(8,128)(2,1)S(1)} %get-tuple-element.47), channel_id=1, source_target_pairs={{0,2},{2,0},{1,3},{3,1},{4,6},{6,4},{5,7},{7,5},{8,10},{10,8},{9,1... | collective-permute-start | bytes 3145736 | tf_op jit(solution)/shard_map/ppermute | solution.py:507
  31.6 23.8 %collective-permute-start.5 = (bf16[6,16,16,128]{3,2,1,0:T(8,128)(2,1)S(1)}, bf16[6,16,16,128]{3,2,1,0:T(8,128)(2,1)S(1)}, u32[]{:S(2)}, u32[]{:S(2)}) collective-permute-start(bf16[6,16,16,128]{3,2,1,0:T(8,128)(2,1)S(1)} %get-tuple-element.44), channel_id=1, source_target_pairs={{0,4},{4,0},{8,12},{12,8},{1,5},{5,1},{9,13},{13,9},{2,6},{6,2},{1... | collective-permute-start | bytes 1179656 | tf_op jit(solution)/shard_map/ppermute | solution.py:513
  48.2 9.6 %collective-permute-start.4 = (bf16[5,16,16,128]{3,2,1,0:T(8,128)(2,1)S(1)}, bf16[5,16,16,128]{3,2,1,0:T(8,128)(2,1)S(1)}, u32[]{:S(2)}, u32[]{:S(2)}) collective-permute-start(bf16[5,16,16,128]{3,2,1,0:T(8,128)(2,1)S(1)} %get-tuple-element.48), channel_id=1, source_target_pairs={{0,4},{4,0},{8,12},{12,8},{1,5},{5,1},{9,13},{13,9},{2,6},{6,2},{1... | collective-permute-start | bytes 983048 | tf_op jit(solution)/shard_map/ppermute | solution.py:513
  57.8 4.1 %collective-permute-start.6 = (bf16[32,32,512]{2,1,0:T(8,128)(2,1)S(1)}, bf16[32,32,512]{2,1,0:T(8,128)(2,1)S(1)}, u32[]{:S(2)}, u32[]{:S(2)}) collective-permute-start(bf16[32,32,512]{2,1,0:T(8,128)(2,1)S(1)} %collective-permute-done.3.refs_0_), channel_id=1, source_target_pairs={{0,1},{1,0},{2,3},{3,2},{4,5},{5,4},{6,7},{7,6},{8,9},{9,8},{10,11... | collective-permute-start | bytes 3145736 | tf_op jit(solution)/shard_map/ppermute | solution.py:510
  57.8 19.3 %collective-permute-start.8 = (bf16[2,16,16,128]{3,2,1,0:T(8,128)(2,1)S(1)}, bf16[2,16,16,128]{3,2,1,0:T(8,128)(2,1)S(1)}, u32[]{:S(2)}, u32[]{:S(2)}) collective-permute-start(bf16[2,16,16,128]{3,2,1,0:T(8,128)(2,1)S(1)} %get-tuple-element.62), channel_id=1, source_target_pairs={{0,4},{4,0},{8,12},{12,8},{1,5},{5,1},{9,13},{13,9},{2,6},{6,2},{1... | collective-permute-start | bytes 393224 | tf_op jit(solution)/shard_map/ppermute | solution.py:513
  59.3 17.9 %collective-permute-start.7 = (bf16[5,16,16,128]{3,2,1,0:T(8,128)(2,1)S(1)}, bf16[5,16,16,128]{3,2,1,0:T(8,128)(2,1)S(1)}, u32[]{:S(2)}, u32[]{:S(2)}) collective-permute-start(bf16[5,16,16,128]{3,2,1,0:T(8,128)(2,1)S(1)} %add_convert_fusion), channel_id=1, source_target_pairs={{0,8},{4,12},{8,0},{12,4},{1,9},{5,13},{9,1},{13,5},{2,10},{6,14},... | collective-permute-start | bytes 983048 | tf_op jit(solution)/shard_map/ppermute | solution.py:513
  74.4 13.5 %collective-permute-start.9 = (bf16[4,16,16,128]{3,2,1,0:T(8,128)(2,1)S(1)}, bf16[4,16,16,128]{3,2,1,0:T(8,128)(2,1)S(1)}, u32[]{:S(2)}, u32[]{:S(2)}) collective-permute-start(bf16[4,16,16,128]{3,2,1,0:T(8,128)(2,1)S(1)} %get-tuple-element.59), channel_id=1, source_target_pairs={{0,4},{4,0},{8,12},{12,8},{1,5},{5,1},{9,13},{13,9},{2,6},{6,2},{1... | collective-permute-start | bytes 786440 | tf_op jit(solution)/shard_map/ppermute | solution.py:513
  75.2 12.8 %collective-permute-start.10 = (bf16[3,16,16,128]{3,2,1,0:T(8,128)(2,1)S(1)}, bf16[3,16,16,128]{3,2,1,0:T(8,128)(2,1)S(1)}, u32[]{:S(2)}, u32[]{:S(2)}) collective-permute-start(bf16[3,16,16,128]{3,2,1,0:T(8,128)(2,1)S(1)} %add_convert_fusion.2), channel_id=1, source_target_pairs={{0,8},{4,12},{8,0},{12,4},{1,9},{5,13},{9,1},{13,5},{2,10},{6,14},... | collective-permute-start | bytes 589832 | tf_op jit(solution)/shard_map/ppermute | solution.py:513
  81.2 15.7 %collective-permute-start.11 = (bf16[4,16,16,128]{3,2,1,0:T(8,128)(2,1)S(1)}, bf16[4,16,16,128]{3,2,1,0:T(8,128)(2,1)S(1)}, u32[]{:S(2)}, u32[]{:S(2)}) collective-permute-start(bf16[4,16,16,128]{3,2,1,0:T(8,128)(2,1)S(1)} %pad_maximum_fusion), channel_id=1, source_target_pairs={{0,4},{4,0},{8,12},{12,8},{1,5},{5,1},{9,13},{13,9},{2,6},{6,2},{1... | collective-permute-start | bytes 786440 | tf_op jit(solution)/shard_map/ppermute | solution.py:513
  87.9 14.5 %collective-permute-start.13 = (bf16[4,16,16,128]{3,2,1,0:T(8,128)(2,1)S(1)}, bf16[4,16,16,128]{3,2,1,0:T(8,128)(2,1)S(1)}, u32[]{:S(2)}, u32[]{:S(2)}) collective-permute-start(bf16[4,16,16,128]{3,2,1,0:T(8,128)(2,1)S(1)} %add_convert_fusion.1), channel_id=1, source_target_pairs={{0,8},{4,12},{8,0},{12,4},{1,9},{5,13},{9,1},{13,5},{2,10},{6,14},... | collective-permute-start | bytes 786440 | tf_op jit(solution)/shard_map/ppermute | solution.py:513
  92.0 10.4 %collective-permute-start.12 = (bf16[3,16,16,128]{3,2,1,0:T(8,128)(2,1)S(1)}, bf16[3,16,16,128]{3,2,1,0:T(8,128)(2,1)S(1)}, u32[]{:S(2)}, u32[]{:S(2)}) collective-permute-start(bf16[3,16,16,128]{3,2,1,0:T(8,128)(2,1)S(1)} %get-tuple-element.70), channel_id=1, source_target_pairs={{0,4},{4,0},{8,12},{12,8},{1,5},{5,1},{9,13},{13,9},{2,6},{6,2},{1... | collective-permute-start | bytes 589832 | tf_op jit(solution)/shard_map/ppermute | solution.py:513
